TPU v7x, 32 devices: a whole 2x2x4 slice. The times are simulated.
32 devices in a mesh: seq: 16 (over z, x, core), tp: 2 (over y).
Axes of the slice: x: 2, y: 2, z: 4, core: 2. Of those that a mesh axis runs over, the one named last changes fastest.
Arguments:
- tokens: bfloat16 [2048, 2560], P('seq', 'tp'), may hold values from -6 to 6
- seg_ids: int32 [2048], P('seq'), may hold values from 0 to 3, never falling along the last dimension, each value on 1 to 1024 neighbouring positions
- norm_gain: bfloat16 [2560], replicated, may hold values from 0.099609375 to 1.8984375
- w_query: bfloat16 [2560, 2048], P('seq', 'tp'), may hold values from -3 to 3
- w_keyval: bfloat16 [2560, 512], P('seq'), may hold values from -1 to 1
- w_out: bfloat16 [2048, 2560], P('tp', 'seq'), may hold values from -0.125 to 0.125
Outputs:
- hidden: bfloat16 [2048, 2560], P('seq', 'tp')
- kv_cache: bfloat16 [2048, 512], P('seq')
Inputs may be any that keep to these rules, and one draw needn't show every extreme that they name: `seg_ids`: ids never fall along the stream; each of the 4 requests holds 1 to 1024 consecutive tokens, one exactly 1024.
All inputs are finite; a program needn't handle non-finite values.
Results may differ from a plain program's by a relative error of at most 0.0085.
Values may be sent and summed in bfloat16 or wider, within the bound.
A program may use at most 64 MiB of HBM per device.

v0:
```python
import jax
import jax.numpy as jnp
from jax import lax
from jax.sharding import PartitionSpec as P

HD = 256
WINDOW = 2048
SEG_MEAN = 512


def from_behind(x, axis, by):
    devices = lax.axis_size(axis)
    pairs = [(i, i + by) for i in range(devices) if 0 <= i + by < devices]
    return lax.ppermute(x, axis, pairs)


def rms_norm(values, gain):
    wide = values.astype(jnp.float32)
    scaled = wide * lax.rsqrt(jnp.mean(wide * wide, axis=-1, keepdims=True) + 1e-06)
    return (scaled * gain.astype(jnp.float32)).astype(jnp.bfloat16)


def rotate(tensor, positions):
    quarter = tensor.shape[-1] // 4
    freq = 10000.0 ** (-jnp.arange(quarter, dtype=jnp.float32) / quarter)
    angle = positions[:, None, None] * freq
    cosine = jnp.cos(angle)
    sine = jnp.sin(angle)
    first = tensor[..., :quarter]
    second = tensor[..., quarter : 2 * quarter]
    return jnp.concatenate(
        [
            first * cosine - second * sine,
            second * cosine + first * sine,
            tensor[..., 2 * quarter :],
        ],
        axis=-1,
    )


def per_device(tokens, seg_ids, norm_gain, w_query, w_keyval, w_out):
    tok_rows = tokens.shape[0]
    seq_count = lax.axis_size("seq")
    my_index = lax.axis_index("seq")
    gathered = lax.all_gather(tokens, "tp", axis=1, tiled=True)
    normed = rms_norm(gathered, norm_gain)
    seg_total = tok_rows * seq_count // SEG_MEAN
    labels = jnp.arange(seg_total, dtype=jnp.int32)
    below = jnp.sum((seg_ids[None, :] < labels[:, None]).astype(jnp.int32), axis=1)
    starts = lax.psum(below, "seq")
    own_start = jnp.sum(jnp.where(seg_ids[:, None] == labels[None, :], starts[None, :], 0), axis=1)
    token_index = my_index * tok_rows + jnp.arange(tok_rows, dtype=jnp.int32)
    positions = (token_index - own_start).astype(jnp.float32)
    query_raw = jnp.dot(
        normed,
        lax.all_gather(w_query, "seq", axis=0, tiled=True),
        preferred_element_type=jnp.float32,
    )
    keyval_raw = jnp.dot(
        normed,
        lax.all_gather(w_keyval, "seq", axis=0, tiled=True),
        preferred_element_type=jnp.float32,
    )
    local_heads = w_query.shape[1] // HD
    queries = rotate(query_raw.reshape(tok_rows, local_heads, HD), positions).astype(jnp.bfloat16)
    key_rows = rotate(keyval_raw[:, None, :HD], positions)[:, 0, :]
    kv_cache = jnp.concatenate([key_rows, keyval_raw[:, HD:]], axis=1).astype(jnp.bfloat16)
    reach = min(WINDOW // tok_rows, seq_count - 1)

    def advance(counter, state):
        current, current_seg, store, store_seg = state
        current, current_seg = from_behind((current, current_seg), "seq", 1)
        slot = reach - 1 - counter
        store = lax.dynamic_update_slice_in_dim(store, current[None], slot, 0)
        store_seg = lax.dynamic_update_slice_in_dim(store_seg, current_seg[None], slot, 0)
        return (current, current_seg, store, store_seg)

    store_init = jnp.zeros((reach, tok_rows, kv_cache.shape[1]), jnp.bfloat16)
    seg_init = jnp.zeros((reach, tok_rows), jnp.int32)
    final_state = lax.fori_loop(0, reach, advance, (kv_cache, seg_ids, store_init, seg_init))
    block_kv = jnp.concatenate(
        [final_state[2].reshape(reach * tok_rows, kv_cache.shape[1]), kv_cache], axis=0
    )
    block_seg = jnp.concatenate([final_state[3].reshape(reach * tok_rows), seg_ids], axis=0)
    key_index = (my_index - reach) * tok_rows + jnp.arange((reach + 1) * tok_rows, dtype=jnp.int32)
    live = (block_seg[None, :] == seg_ids[:, None]) & (key_index[None, :] <= token_index[:, None])
    live = live & (token_index[:, None] - key_index[None, :] < WINDOW) & (key_index[None, :] >= 0)
    all_keys = block_kv[:, :HD]
    all_values = block_kv[:, HD:]
    head_outputs = []
    for head_idx in range(local_heads):
        scores = lax.dot_general(
            queries[:, head_idx, :],
            all_keys,
            (((1,), (1,)), ((), ())),
            preferred_element_type=jnp.float32,
        ) * HD ** (-0.5)
        scores = jnp.where(live, scores, -1e30)
        peak = jnp.max(scores, axis=1, keepdims=True)
        powered = jnp.exp(scores - peak)
        weights = (powered / jnp.sum(powered, axis=1, keepdims=True)).astype(jnp.bfloat16)
        head_outputs.append(
            jnp.dot(weights, all_values, preferred_element_type=jnp.float32).astype(jnp.bfloat16)
        )
    attended = jnp.concatenate(head_outputs, axis=1)
    partial_value = jnp.dot(
        attended,
        lax.all_gather(w_out, "seq", axis=1, tiled=True),
        preferred_element_type=jnp.float32,
    )
    summed = lax.psum_scatter(
        partial_value.astype(jnp.bfloat16), "tp", scatter_dimension=1, tiled=True
    ).astype(jnp.float32)
    hidden = (tokens.astype(jnp.float32) + summed).astype(jnp.bfloat16)
    return (hidden, kv_cache)


def solution(mesh):
    in_specs = (P("seq", "tp"), P("seq"), P(), P("seq", "tp"), P("seq", None), P("tp", "seq"))
    out_specs = (P("seq", "tp"), P("seq", None))
    return jax.shard_map(
        per_device, mesh=mesh, in_specs=in_specs, out_specs=out_specs, check_vma=False
    )
```

profile of v0, /device:TPU:0, one launch (start us, length us, event | category | flops | bytes accessed | tf_op | source)
XLA Modules:
  0.0 244.8 jit_solution(7832263908713972242)
XLA Ops:
  10.2 13.8 %psum.7 = s32[4]{0:T(128)S(1)} all-reduce(s32[4]{0:T(128)S(1)} %convert_reduce_fusion), channel_id=1, replica_groups=mesh['seq'=16,'tp'=2] {'seq'}, use_global_device_ids=true, to_apply=%region_2.0 | all-reduce | flops 4 | bytes 32 | tf_op jit(solution)/shard_map/psum | solution.py:50
  25.5 8.0 %all_gather.12 = bf16[128,2560]{1,0:T(8,128)(2,1)S(1)} all-gather(bf16[128,1280]{1,0:T(8,128)(2,1)} %param.8), channel_id=1, replica_groups=mesh['seq'=16,'tp'=2] {'tp'}, dimensions={1}, use_global_device_ids=true | all-gather | bytes 983040 | tf_op jit(solution)/shard_map/all_gather | solution.py:45
  34.0 22.2 %all-gather.4.cloned.1.call-done = bf16[2560,512]{1,0:T(8,128)(2,1)} async-done(((bf16[160,512]{1,0:T(8,128)(2,1)}), bf16[2560,512]{1,0:T(8,128)(2,1)}) %all-gather.4.cloned.1.call-update) | async-done | bytes 2621456 | tf_op jit(solution)/shard_map/all_gather | solution.py:61
  56.2 2.9 %fusion.31 = f32[128,512]{0,1:T(8,128)S(1)} fusion(bf16[2560,512]{1,0:T(8,128)(2,1)} %all-gather.4.cloned.1.call-done, bf16[128,2560]{1,0:T(8,128)(2,1)S(1)} %all_gather.12, f32[2560]{0:T(1024)S(1)} %convert_element_type.59, f32[128]{0:T(128)S(1)} %add_rsqrt_fusion), kind=kOutput, calls=%fused_computation.59 | convolution fusion | flops 336855040 | bytes 3549696 | tf_op jit(solution)/shard_map/dot_general | solution.py:59
  59.8 139.2 %while.19 = (s32[]{:T(128)}, bf16[128,512]{1,0:T(8,128)(2,1)S(1)}, s32[128]{0:T(128)S(1)}, bf16[15,128,512]{2,1,0:T(8,128)(2,1)S(1)}, s32[15,128]{1,0:T(8,128)S(...) while((s32[]{:T(128)}, bf16[128,512]{1,0:T(8,128)(2,1)S(1)}, s32[128]{0:T(128)S(1)}, ...), condition=%wide.region_5.6_spmd, body=%wide.region_4.5_spmd.sunk | while | flops 6 | bytes 1052899 | solution.py:80
  67.4 4.0 %collective-permute-start.1 = (s32[128]{0:T(128)S(1)}, s32[128]{0:T(128)S(1)}, u32[]{:S(2)}, u32[]{:S(2)}) collective-permute-start(s32[128]{0:T(128)S(1)} %get-tuple-element.178), channel_id=1, source_target_pairs={{0,2},{2,4},{4,6},{6,8},{8,10},{10,12},{12,14},{14,16},{16,18},{18... | collective-permute-start | bytes 1544 | tf_op jit(solution)/shard_map/while/body/eval_jaxpr/ppermute | solution.py:14
  74.6 4.8 %collective-permute-start.1 = (s32[128]{0:T(128)S(1)}, s32[128]{0:T(128)S(1)}, u32[]{:S(2)}, u32[]{:S(2)}) collective-permute-start(s32[128]{0:T(128)S(1)} %get-tuple-element.178), channel_id=1, source_target_pairs={{0,2},{2,4},{4,6},{6,8},{8,10},{10,12},{12,14},{14,16},{16,18},{18... | collective-permute-start | bytes 1544 | tf_op jit(solution)/shard_map/while/body/eval_jaxpr/ppermute | solution.py:14
  80.3 3.6 %collective-permute-start = (bf16[128,512]{1,0:T(8,128)(2,1)S(1)}, bf16[128,512]{1,0:T(8,128)(2,1)S(1)}, u32[]{:S(2)}, u32[]{:S(2)}) collective-permute-start(bf16[128,512]{1,0:T(8,128)(2,1)S(1)} %get-tuple-element.177), channel_id=1, source_target_pairs={{0,2},{2,4},{4,6},{6,8},{8,10},{10,12},{12,14},{14,16},{16,18},{18... | collective-permute-start | bytes 393224 | tf_op jit(solution)/shard_map/while/body/eval_jaxpr/ppermute | solution.py:14
  83.9 5.4 %collective-permute-start.1 = (s32[128]{0:T(128)S(1)}, s32[128]{0:T(128)S(1)}, u32[]{:S(2)}, u32[]{:S(2)}) collective-permute-start(s32[128]{0:T(128)S(1)} %get-tuple-element.178), channel_id=1, source_target_pairs={{0,2},{2,4},{4,6},{6,8},{8,10},{10,12},{12,14},{14,16},{16,18},{18... | collective-permute-start | bytes 1544 | tf_op jit(solution)/shard_map/while/body/eval_jaxpr/ppermute | solution.py:14
  90.2 3.9 %collective-permute-start = (bf16[128,512]{1,0:T(8,128)(2,1)S(1)}, bf16[128,512]{1,0:T(8,128)(2,1)S(1)}, u32[]{:S(2)}, u32[]{:S(2)}) collective-permute-start(bf16[128,512]{1,0:T(8,128)(2,1)S(1)} %get-tuple-element.177), channel_id=1, source_target_pairs={{0,2},{2,4},{4,6},{6,8},{8,10},{10,12},{12,14},{14,16},{16,18},{18... | collective-permute-start | bytes 393224 | tf_op jit(solution)/shard_map/while/body/eval_jaxpr/ppermute | solution.py:14
  94.1 4.4 %collective-permute-start.1 = (s32[128]{0:T(128)S(1)}, s32[128]{0:T(128)S(1)}, u32[]{:S(2)}, u32[]{:S(2)}) collective-permute-start(s32[128]{0:T(128)S(1)} %get-tuple-element.178), channel_id=1, source_target_pairs={{0,2},{2,4},{4,6},{6,8},{8,10},{10,12},{12,14},{14,16},{16,18},{18... | collective-permute-start | bytes 1544 | tf_op jit(solution)/shard_map/while/body/eval_jaxpr/ppermute | solution.py:14
  99.4 3.9 %collective-permute-start = (bf16[128,512]{1,0:T(8,128)(2,1)S(1)}, bf16[128,512]{1,0:T(8,128)(2,1)S(1)}, u32[]{:S(2)}, u32[]{:S(2)}) collective-permute-start(bf16[128,512]{1,0:T(8,128)(2,1)S(1)} %get-tuple-element.177), channel_id=1, source_target_pairs={{0,2},{2,4},{4,6},{6,8},{8,10},{10,12},{12,14},{14,16},{16,18},{18... | collective-permute-start | bytes 393224 | tf_op jit(solution)/shard_map/while/body/eval_jaxpr/ppermute | solution.py:14
  103.3 4.4 %collective-permute-start.1 = (s32[128]{0:T(128)S(1)}, s32[128]{0:T(128)S(1)}, u32[]{:S(2)}, u32[]{:S(2)}) collective-permute-start(s32[128]{0:T(128)S(1)} %get-tuple-element.178), channel_id=1, source_target_pairs={{0,2},{2,4},{4,6},{6,8},{8,10},{10,12},{12,14},{14,16},{16,18},{18... | collective-permute-start | bytes 1544 | tf_op jit(solution)/shard_map/while/body/eval_jaxpr/ppermute | solution.py:14
  111.4 5.4 %collective-permute-start.1 = (s32[128]{0:T(128)S(1)}, s32[128]{0:T(128)S(1)}, u32[]{:S(2)}, u32[]{:S(2)}) collective-permute-start(s32[128]{0:T(128)S(1)} %get-tuple-element.178), channel_id=1, source_target_pairs={{0,2},{2,4},{4,6},{6,8},{8,10},{10,12},{12,14},{14,16},{16,18},{18... | collective-permute-start | bytes 1544 | tf_op jit(solution)/shard_map/while/body/eval_jaxpr/ppermute | solution.py:14
  117.7 3.6 %collective-permute-start = (bf16[128,512]{1,0:T(8,128)(2,1)S(1)}, bf16[128,512]{1,0:T(8,128)(2,1)S(1)}, u32[]{:S(2)}, u32[]{:S(2)}) collective-permute-start(bf16[128,512]{1,0:T(8,128)(2,1)S(1)} %get-tuple-element.177), channel_id=1, source_target_pairs={{0,2},{2,4},{4,6},{6,8},{8,10},{10,12},{12,14},{14,16},{16,18},{18... | collective-permute-start | bytes 393224 | tf_op jit(solution)/shard_map/while/body/eval_jaxpr/ppermute | solution.py:14
  121.2 5.4 %collective-permute-start.1 = (s32[128]{0:T(128)S(1)}, s32[128]{0:T(128)S(1)}, u32[]{:S(2)}, u32[]{:S(2)}) collective-permute-start(s32[128]{0:T(128)S(1)} %get-tuple-element.178), channel_id=1, source_target_pairs={{0,2},{2,4},{4,6},{6,8},{8,10},{10,12},{12,14},{14,16},{16,18},{18... | collective-permute-start | bytes 1544 | tf_op jit(solution)/shard_map/while/body/eval_jaxpr/ppermute | solution.py:14
  127.5 3.1 %collective-permute-start = (bf16[128,512]{1,0:T(8,128)(2,1)S(1)}, bf16[128,512]{1,0:T(8,128)(2,1)S(1)}, u32[]{:S(2)}, u32[]{:S(2)}) collective-permute-start(bf16[128,512]{1,0:T(8,128)(2,1)S(1)} %get-tuple-element.177), channel_id=1, source_target_pairs={{0,2},{2,4},{4,6},{6,8},{8,10},{10,12},{12,14},{14,16},{16,18},{18... | collective-permute-start | bytes 393224 | tf_op jit(solution)/shard_map/while/body/eval_jaxpr/ppermute | solution.py:14
  130.7 5.8 %collective-permute-start.1 = (s32[128]{0:T(128)S(1)}, s32[128]{0:T(128)S(1)}, u32[]{:S(2)}, u32[]{:S(2)}) collective-permute-start(s32[128]{0:T(128)S(1)} %get-tuple-element.178), channel_id=1, source_target_pairs={{0,2},{2,4},{4,6},{6,8},{8,10},{10,12},{12,14},{14,16},{16,18},{18... | collective-permute-start | bytes 1544 | tf_op jit(solution)/shard_map/while/body/eval_jaxpr/ppermute | solution.py:14
  137.3 3.6 %collective-permute-start = (bf16[128,512]{1,0:T(8,128)(2,1)S(1)}, bf16[128,512]{1,0:T(8,128)(2,1)S(1)}, u32[]{:S(2)}, u32[]{:S(2)}) collective-permute-start(bf16[128,512]{1,0:T(8,128)(2,1)S(1)} %get-tuple-element.177), channel_id=1, source_target_pairs={{0,2},{2,4},{4,6},{6,8},{8,10},{10,12},{12,14},{14,16},{16,18},{18... | collective-permute-start | bytes 393224 | tf_op jit(solution)/shard_map/while/body/eval_jaxpr/ppermute | solution.py:14
  141.0 5.4 %collective-permute-start.1 = (s32[128]{0:T(128)S(1)}, s32[128]{0:T(128)S(1)}, u32[]{:S(2)}, u32[]{:S(2)}) collective-permute-start(s32[128]{0:T(128)S(1)} %get-tuple-element.178), channel_id=1, source_target_pairs={{0,2},{2,4},{4,6},{6,8},{8,10},{10,12},{12,14},{14,16},{16,18},{18... | collective-permute-start | bytes 1544 | tf_op jit(solution)/shard_map/while/body/eval_jaxpr/ppermute | solution.py:14
  149.5 4.9 %collective-permute-start.1 = (s32[128]{0:T(128)S(1)}, s32[128]{0:T(128)S(1)}, u32[]{:S(2)}, u32[]{:S(2)}) collective-permute-start(s32[128]{0:T(128)S(1)} %get-tuple-element.178), channel_id=1, source_target_pairs={{0,2},{2,4},{4,6},{6,8},{8,10},{10,12},{12,14},{14,16},{16,18},{18... | collective-permute-start | bytes 1544 | tf_op jit(solution)/shard_map/while/body/eval_jaxpr/ppermute | solution.py:14
  155.3 3.9 %collective-permute-start = (bf16[128,512]{1,0:T(8,128)(2,1)S(1)}, bf16[128,512]{1,0:T(8,128)(2,1)S(1)}, u32[]{:S(2)}, u32[]{:S(2)}) collective-permute-start(bf16[128,512]{1,0:T(8,128)(2,1)S(1)} %get-tuple-element.177), channel_id=1, source_target_pairs={{0,2},{2,4},{4,6},{6,8},{8,10},{10,12},{12,14},{14,16},{16,18},{18... | collective-permute-start | bytes 393224 | tf_op jit(solution)/shard_map/while/body/eval_jaxpr/ppermute | solution.py:14
  159.2 5.9 %collective-permute-start.1 = (s32[128]{0:T(128)S(1)}, s32[128]{0:T(128)S(1)}, u32[]{:S(2)}, u32[]{:S(2)}) collective-permute-start(s32[128]{0:T(128)S(1)} %get-tuple-element.178), channel_id=1, source_target_pairs={{0,2},{2,4},{4,6},{6,8},{8,10},{10,12},{12,14},{14,16},{16,18},{18... | collective-permute-start | bytes 1544 | tf_op jit(solution)/shard_map/while/body/eval_jaxpr/ppermute | solution.py:14
  166.0 3.8 %collective-permute-start = (bf16[128,512]{1,0:T(8,128)(2,1)S(1)}, bf16[128,512]{1,0:T(8,128)(2,1)S(1)}, u32[]{:S(2)}, u32[]{:S(2)}) collective-permute-start(bf16[128,512]{1,0:T(8,128)(2,1)S(1)} %get-tuple-element.177), channel_id=1, source_target_pairs={{0,2},{2,4},{4,6},{6,8},{8,10},{10,12},{12,14},{14,16},{16,18},{18... | collective-permute-start | bytes 393224 | tf_op jit(solution)/shard_map/while/body/eval_jaxpr/ppermute | solution.py:14
  169.9 5.4 %collective-permute-start.1 = (s32[128]{0:T(128)S(1)}, s32[128]{0:T(128)S(1)}, u32[]{:S(2)}, u32[]{:S(2)}) collective-permute-start(s32[128]{0:T(128)S(1)} %get-tuple-element.178), channel_id=1, source_target_pairs={{0,2},{2,4},{4,6},{6,8},{8,10},{10,12},{12,14},{14,16},{16,18},{18... | collective-permute-start | bytes 1544 | tf_op jit(solution)/shard_map/while/body/eval_jaxpr/ppermute | solution.py:14
  176.2 3.9 %collective-permute-start = (bf16[128,512]{1,0:T(8,128)(2,1)S(1)}, bf16[128,512]{1,0:T(8,128)(2,1)S(1)}, u32[]{:S(2)}, u32[]{:S(2)}) collective-permute-start(bf16[128,512]{1,0:T(8,128)(2,1)S(1)} %get-tuple-element.177), channel_id=1, source_target_pairs={{0,2},{2,4},{4,6},{6,8},{8,10},{10,12},{12,14},{14,16},{16,18},{18... | collective-permute-start | bytes 393224 | tf_op jit(solution)/shard_map/while/body/eval_jaxpr/ppermute | solution.py:14
  180.1 6.0 %collective-permute-start.1 = (s32[128]{0:T(128)S(1)}, s32[128]{0:T(128)S(1)}, u32[]{:S(2)}, u32[]{:S(2)}) collective-permute-start(s32[128]{0:T(128)S(1)} %get-tuple-element.178), channel_id=1, source_target_pairs={{0,2},{2,4},{4,6},{6,8},{8,10},{10,12},{12,14},{14,16},{16,18},{18... | collective-permute-start | bytes 1544 | tf_op jit(solution)/shard_map/while/body/eval_jaxpr/ppermute | solution.py:14
  187.0 4.9 %collective-permute-start = (bf16[128,512]{1,0:T(8,128)(2,1)S(1)}, bf16[128,512]{1,0:T(8,128)(2,1)S(1)}, u32[]{:S(2)}, u32[]{:S(2)}) collective-permute-start(bf16[128,512]{1,0:T(8,128)(2,1)S(1)} %get-tuple-element.177), channel_id=1, source_target_pairs={{0,2},{2,4},{4,6},{6,8},{8,10},{10,12},{12,14},{14,16},{16,18},{18... | collective-permute-start | bytes 393224 | tf_op jit(solution)/shard_map/while/body/eval_jaxpr/ppermute | solution.py:14
  191.9 6.2 %collective-permute-start.1 = (s32[128]{0:T(128)S(1)}, s32[128]{0:T(128)S(1)}, u32[]{:S(2)}, u32[]{:S(2)}) collective-permute-start(s32[128]{0:T(128)S(1)} %get-tuple-element.178), channel_id=1, source_target_pairs={{0,2},{2,4},{4,6},{6,8},{8,10},{10,12},{12,14},{14,16},{16,18},{18... | collective-permute-start | bytes 1544 | tf_op jit(solution)/shard_map/while/body/eval_jaxpr/ppermute | solution.py:14
  200.5 3.4 %fusion.29 = f32[128,1024]{1,0:T(8,128)S(1)} fusion(bf16[2560,1024]{1,0:T(8,128)(2,1)} %all-gather.6.cloned.1.call-done, bf16[128,2560]{1,0:T(8,128)(2,1)S(1)} %all_gather.12, f32[2560]{0:T(1024)S(1)} %convert_element_type.59, f32[128]{0:T(128)S(1)} %add_rsqrt_fusion), kind=kOutput, calls=%fused_computation.58 | convolution fusion | flops 672399360 | bytes 6433280 | tf_op jit(solution)/shard_map/dot_general | solution.py:54
  211.0 5.2 %convolution_convert_fusion = bf16[128,2560]{1,0:T(8,128)(2,1)} fusion(bf16[1024,2560]{0,1:T(8,128)(2,1)} %all-gather.8.cloned.1.call-done, bf16[128,256]{1,0:T(8,128)(2,1)S(1)} %convolution_convert_fusion.1, bf16[128,256]{1,0:T(8,128)(2,1)S(1)} %convolution_convert_fusion.2, bf16[128,256]{1,0:T(8,128)(2,1)S(1)} %convolution_convert_fusion.3, ...), kind=kOutput, calls=%fused_computation.1 | convolution fusion | flops 672464896 | bytes 6160384 | tf_op jit(solution)/shard_map/dot_general | solution.py:106
  216.3 20.2 %reduce-scatter.2.cloned.1.call-done = bf16[128,1280]{1,0:T(8,128)(2,1)} async-done(((bf16[128,2560]{1,0:T(8,128)(2,1)}), bf16[128,1280]{1,0:T(8,128)(2,1)}) %reduce-scatter.2.cloned.1.call-update) | async-done | bytes 327696 | tf_op jit(solution)/shard_map/reduce_scatter | solution.py:111
  (159 shorter events, 42.4 us)
Async XLA Ops:
  7.2 49.0 %all-gather.4.cloned.1.call-start = ((), (), s32[]{:S(2)}) async-start(), calls=%async_computation.1 | async-start | bytes 2785280 | tf_op jit(solution)/shard_map/all_gather | solution.py:61
  7.9 192.6 %all-gather.6.cloned.1.call-start = ((), (), s32[]{:S(2)}) async-start(), calls=%async_computation.2 | async-start | bytes 5570560 | tf_op jit(solution)/shard_map/all_gather | solution.py:56
  8.6 202.3 %all-gather.8.cloned.1.call-start = ((), (), s32[]{:S(2)}) async-start(), calls=%async_computation.3 | async-start | bytes 5570560 | tf_op jit(solution)/shard_map/all_gather | solution.py:108
  9.4 227.1 %reduce-scatter.2.cloned.1.call-start = ((), (), s32[]{:S(2)}) async-start(), calls=%async_computation.4 | async-start | bytes 983040 | tf_op jit(solution)/shard_map/reduce_scatter | solution.py:111
  59.8 5.3 %collective-permute-start = (bf16[128,512]{1,0:T(8,128)(2,1)S(1)}, bf16[128,512]{1,0:T(8,128)(2,1)S(1)}, u32[]{:S(2)}, u32[]{:S(2)}) collective-permute-start(bf16[128,512]{1,0:T(8,128)(2,1)S(1)} %get-tuple-element.177), channel_id=1, source_target_pairs={{0,2},{2,4},{4,6},{6,8},{8,10},{10,12},{12,14},{14,16},{16,18},{18... | collective-permute-start | bytes 393224 | tf_op jit(solution)/shard_map/while/body/eval_jaxpr/ppermute | solution.py:14
  65.2 7.1 %collective-permute-start = (bf16[128,512]{1,0:T(8,128)(2,1)S(1)}, bf16[128,512]{1,0:T(8,128)(2,1)S(1)}, u32[]{:S(2)}, u32[]{:S(2)}) collective-permute-start(bf16[128,512]{1,0:T(8,128)(2,1)S(1)} %get-tuple-element.177), channel_id=1, source_target_pairs={{0,2},{2,4},{4,6},{6,8},{8,10},{10,12},{12,14},{14,16},{16,18},{18... | collective-permute-start | bytes 393224 | tf_op jit(solution)/shard_map/while/body/eval_jaxpr/ppermute | solution.py:14
  72.3 7.9 %collective-permute-start = (bf16[128,512]{1,0:T(8,128)(2,1)S(1)}, bf16[128,512]{1,0:T(8,128)(2,1)S(1)}, u32[]{:S(2)}, u32[]{:S(2)}) collective-permute-start(bf16[128,512]{1,0:T(8,128)(2,1)S(1)} %get-tuple-element.177), channel_id=1, source_target_pairs={{0,2},{2,4},{4,6},{6,8},{8,10},{10,12},{12,14},{14,16},{16,18},{18... | collective-permute-start | bytes 393224 | tf_op jit(solution)/shard_map/while/body/eval_jaxpr/ppermute | solution.py:14
  74.6 5.6 %collective-permute-start.1 = (s32[128]{0:T(128)S(1)}, s32[128]{0:T(128)S(1)}, u32[]{:S(2)}, u32[]{:S(2)}) collective-permute-start(s32[128]{0:T(128)S(1)} %get-tuple-element.178), channel_id=1, source_target_pairs={{0,2},{2,4},{4,6},{6,8},{8,10},{10,12},{12,14},{14,16},{16,18},{18... | collective-permute-start | bytes 1544 | tf_op jit(solution)/shard_map/while/body/eval_jaxpr/ppermute | solution.py:14
  80.3 9.9 %collective-permute-start = (bf16[128,512]{1,0:T(8,128)(2,1)S(1)}, bf16[128,512]{1,0:T(8,128)(2,1)S(1)}, u32[]{:S(2)}, u32[]{:S(2)}) collective-permute-start(bf16[128,512]{1,0:T(8,128)(2,1)S(1)} %get-tuple-element.177), channel_id=1, source_target_pairs={{0,2},{2,4},{4,6},{6,8},{8,10},{10,12},{12,14},{14,16},{16,18},{18... | collective-permute-start | bytes 393224 | tf_op jit(solution)/shard_map/while/body/eval_jaxpr/ppermute | solution.py:14
  83.9 6.2 %collective-permute-start.1 = (s32[128]{0:T(128)S(1)}, s32[128]{0:T(128)S(1)}, u32[]{:S(2)}, u32[]{:S(2)}) collective-permute-start(s32[128]{0:T(128)S(1)} %get-tuple-element.178), channel_id=1, source_target_pairs={{0,2},{2,4},{4,6},{6,8},{8,10},{10,12},{12,14},{14,16},{16,18},{18... | collective-permute-start | bytes 1544 | tf_op jit(solution)/shard_map/while/body/eval_jaxpr/ppermute | solution.py:14
  90.2 9.2 %collective-permute-start = (bf16[128,512]{1,0:T(8,128)(2,1)S(1)}, bf16[128,512]{1,0:T(8,128)(2,1)S(1)}, u32[]{:S(2)}, u32[]{:S(2)}) collective-permute-start(bf16[128,512]{1,0:T(8,128)(2,1)S(1)} %get-tuple-element.177), channel_id=1, source_target_pairs={{0,2},{2,4},{4,6},{6,8},{8,10},{10,12},{12,14},{14,16},{16,18},{18... | collective-permute-start | bytes 393224 | tf_op jit(solution)/shard_map/while/body/eval_jaxpr/ppermute | solution.py:14
  94.1 5.2 %collective-permute-start.1 = (s32[128]{0:T(128)S(1)}, s32[128]{0:T(128)S(1)}, u32[]{:S(2)}, u32[]{:S(2)}) collective-permute-start(s32[128]{0:T(128)S(1)} %get-tuple-element.178), channel_id=1, source_target_pairs={{0,2},{2,4},{4,6},{6,8},{8,10},{10,12},{12,14},{14,16},{16,18},{18... | collective-permute-start | bytes 1544 | tf_op jit(solution)/shard_map/while/body/eval_jaxpr/ppermute | solution.py:14
  99.4 9.2 %collective-permute-start = (bf16[128,512]{1,0:T(8,128)(2,1)S(1)}, bf16[128,512]{1,0:T(8,128)(2,1)S(1)}, u32[]{:S(2)}, u32[]{:S(2)}) collective-permute-start(bf16[128,512]{1,0:T(8,128)(2,1)S(1)} %get-tuple-element.177), channel_id=1, source_target_pairs={{0,2},{2,4},{4,6},{6,8},{8,10},{10,12},{12,14},{14,16},{16,18},{18... | collective-permute-start | bytes 393224 | tf_op jit(solution)/shard_map/while/body/eval_jaxpr/ppermute | solution.py:14
  103.3 5.2 %collective-permute-start.1 = (s32[128]{0:T(128)S(1)}, s32[128]{0:T(128)S(1)}, u32[]{:S(2)}, u32[]{:S(2)}) collective-permute-start(s32[128]{0:T(128)S(1)} %get-tuple-element.178), channel_id=1, source_target_pairs={{0,2},{2,4},{4,6},{6,8},{8,10},{10,12},{12,14},{14,16},{16,18},{18... | collective-permute-start | bytes 1544 | tf_op jit(solution)/shard_map/while/body/eval_jaxpr/ppermute | solution.py:14
  108.7 8.9 %collective-permute-start = (bf16[128,512]{1,0:T(8,128)(2,1)S(1)}, bf16[128,512]{1,0:T(8,128)(2,1)S(1)}, u32[]{:S(2)}, u32[]{:S(2)}) collective-permute-start(bf16[128,512]{1,0:T(8,128)(2,1)S(1)} %get-tuple-element.177), channel_id=1, source_target_pairs={{0,2},{2,4},{4,6},{6,8},{8,10},{10,12},{12,14},{14,16},{16,18},{18... | collective-permute-start | bytes 393224 | tf_op jit(solution)/shard_map/while/body/eval_jaxpr/ppermute | solution.py:14
  111.4 6.2 %collective-permute-start.1 = (s32[128]{0:T(128)S(1)}, s32[128]{0:T(128)S(1)}, u32[]{:S(2)}, u32[]{:S(2)}) collective-permute-start(s32[128]{0:T(128)S(1)} %get-tuple-element.178), channel_id=1, source_target_pairs={{0,2},{2,4},{4,6},{6,8},{8,10},{10,12},{12,14},{14,16},{16,18},{18... | collective-permute-start | bytes 1544 | tf_op jit(solution)/shard_map/while/body/eval_jaxpr/ppermute | solution.py:14
  117.7 9.8 %collective-permute-start = (bf16[128,512]{1,0:T(8,128)(2,1)S(1)}, bf16[128,512]{1,0:T(8,128)(2,1)S(1)}, u32[]{:S(2)}, u32[]{:S(2)}) collective-permute-start(bf16[128,512]{1,0:T(8,128)(2,1)S(1)} %get-tuple-element.177), channel_id=1, source_target_pairs={{0,2},{2,4},{4,6},{6,8},{8,10},{10,12},{12,14},{14,16},{16,18},{18... | collective-permute-start | bytes 393224 | tf_op jit(solution)/shard_map/while/body/eval_jaxpr/ppermute | solution.py:14
  121.2 6.2 %collective-permute-start.1 = (s32[128]{0:T(128)S(1)}, s32[128]{0:T(128)S(1)}, u32[]{:S(2)}, u32[]{:S(2)}) collective-permute-start(s32[128]{0:T(128)S(1)} %get-tuple-element.178), channel_id=1, source_target_pairs={{0,2},{2,4},{4,6},{6,8},{8,10},{10,12},{12,14},{14,16},{16,18},{18... | collective-permute-start | bytes 1544 | tf_op jit(solution)/shard_map/while/body/eval_jaxpr/ppermute | solution.py:14
  127.5 9.7 %collective-permute-start = (bf16[128,512]{1,0:T(8,128)(2,1)S(1)}, bf16[128,512]{1,0:T(8,128)(2,1)S(1)}, u32[]{:S(2)}, u32[]{:S(2)}) collective-permute-start(bf16[128,512]{1,0:T(8,128)(2,1)S(1)} %get-tuple-element.177), channel_id=1, source_target_pairs={{0,2},{2,4},{4,6},{6,8},{8,10},{10,12},{12,14},{14,16},{16,18},{18... | collective-permute-start | bytes 393224 | tf_op jit(solution)/shard_map/while/body/eval_jaxpr/ppermute | solution.py:14
  130.7 6.6 %collective-permute-start.1 = (s32[128]{0:T(128)S(1)}, s32[128]{0:T(128)S(1)}, u32[]{:S(2)}, u32[]{:S(2)}) collective-permute-start(s32[128]{0:T(128)S(1)} %get-tuple-element.178), channel_id=1, source_target_pairs={{0,2},{2,4},{4,6},{6,8},{8,10},{10,12},{12,14},{14,16},{16,18},{18... | collective-permute-start | bytes 1544 | tf_op jit(solution)/shard_map/while/body/eval_jaxpr/ppermute | solution.py:14
  137.3 9.9 %collective-permute-start = (bf16[128,512]{1,0:T(8,128)(2,1)S(1)}, bf16[128,512]{1,0:T(8,128)(2,1)S(1)}, u32[]{:S(2)}, u32[]{:S(2)}) collective-permute-start(bf16[128,512]{1,0:T(8,128)(2,1)S(1)} %get-tuple-element.177), channel_id=1, source_target_pairs={{0,2},{2,4},{4,6},{6,8},{8,10},{10,12},{12,14},{14,16},{16,18},{18... | collective-permute-start | bytes 393224 | tf_op jit(solution)/shard_map/while/body/eval_jaxpr/ppermute | solution.py:14
  141.0 6.2 %collective-permute-start.1 = (s32[128]{0:T(128)S(1)}, s32[128]{0:T(128)S(1)}, u32[]{:S(2)}, u32[]{:S(2)}) collective-permute-start(s32[128]{0:T(128)S(1)} %get-tuple-element.178), channel_id=1, source_target_pairs={{0,2},{2,4},{4,6},{6,8},{8,10},{10,12},{12,14},{14,16},{16,18},{18... | collective-permute-start | bytes 1544 | tf_op jit(solution)/shard_map/while/body/eval_jaxpr/ppermute | solution.py:14
  147.3 7.9 %collective-permute-start = (bf16[128,512]{1,0:T(8,128)(2,1)S(1)}, bf16[128,512]{1,0:T(8,128)(2,1)S(1)}, u32[]{:S(2)}, u32[]{:S(2)}) collective-permute-start(bf16[128,512]{1,0:T(8,128)(2,1)S(1)} %get-tuple-element.177), channel_id=1, source_target_pairs={{0,2},{2,4},{4,6},{6,8},{8,10},{10,12},{12,14},{14,16},{16,18},{18... | collective-permute-start | bytes 393224 | tf_op jit(solution)/shard_map/while/body/eval_jaxpr/ppermute | solution.py:14
  149.5 5.7 %collective-permute-start.1 = (s32[128]{0:T(128)S(1)}, s32[128]{0:T(128)S(1)}, u32[]{:S(2)}, u32[]{:S(2)}) collective-permute-start(s32[128]{0:T(128)S(1)} %get-tuple-element.178), channel_id=1, source_target_pairs={{0,2},{2,4},{4,6},{6,8},{8,10},{10,12},{12,14},{14,16},{16,18},{18... | collective-permute-start | bytes 1544 | tf_op jit(solution)/shard_map/while/body/eval_jaxpr/ppermute | solution.py:14
  155.3 10.7 %collective-permute-start = (bf16[128,512]{1,0:T(8,128)(2,1)S(1)}, bf16[128,512]{1,0:T(8,128)(2,1)S(1)}, u32[]{:S(2)}, u32[]{:S(2)}) collective-permute-start(bf16[128,512]{1,0:T(8,128)(2,1)S(1)} %get-tuple-element.177), channel_id=1, source_target_pairs={{0,2},{2,4},{4,6},{6,8},{8,10},{10,12},{12,14},{14,16},{16,18},{18... | collective-permute-start | bytes 393224 | tf_op jit(solution)/shard_map/while/body/eval_jaxpr/ppermute | solution.py:14
  159.2 6.7 %collective-permute-start.1 = (s32[128]{0:T(128)S(1)}, s32[128]{0:T(128)S(1)}, u32[]{:S(2)}, u32[]{:S(2)}) collective-permute-start(s32[128]{0:T(128)S(1)} %get-tuple-element.178), channel_id=1, source_target_pairs={{0,2},{2,4},{4,6},{6,8},{8,10},{10,12},{12,14},{14,16},{16,18},{18... | collective-permute-start | bytes 1544 | tf_op jit(solution)/shard_map/while/body/eval_jaxpr/ppermute | solution.py:14
  166.0 10.1 %collective-permute-start = (bf16[128,512]{1,0:T(8,128)(2,1)S(1)}, bf16[128,512]{1,0:T(8,128)(2,1)S(1)}, u32[]{:S(2)}, u32[]{:S(2)}) collective-permute-start(bf16[128,512]{1,0:T(8,128)(2,1)S(1)} %get-tuple-element.177), channel_id=1, source_target_pairs={{0,2},{2,4},{4,6},{6,8},{8,10},{10,12},{12,14},{14,16},{16,18},{18... | collective-permute-start | bytes 393224 | tf_op jit(solution)/shard_map/while/body/eval_jaxpr/ppermute | solution.py:14
  169.9 6.2 %collective-permute-start.1 = (s32[128]{0:T(128)S(1)}, s32[128]{0:T(128)S(1)}, u32[]{:S(2)}, u32[]{:S(2)}) collective-permute-start(s32[128]{0:T(128)S(1)} %get-tuple-element.178), channel_id=1, source_target_pairs={{0,2},{2,4},{4,6},{6,8},{8,10},{10,12},{12,14},{14,16},{16,18},{18... | collective-permute-start | bytes 1544 | tf_op jit(solution)/shard_map/while/body/eval_jaxpr/ppermute | solution.py:14
  176.2 10.8 %collective-permute-start = (bf16[128,512]{1,0:T(8,128)(2,1)S(1)}, bf16[128,512]{1,0:T(8,128)(2,1)S(1)}, u32[]{:S(2)}, u32[]{:S(2)}) collective-permute-start(bf16[128,512]{1,0:T(8,128)(2,1)S(1)} %get-tuple-element.177), channel_id=1, source_target_pairs={{0,2},{2,4},{4,6},{6,8},{8,10},{10,12},{12,14},{14,16},{16,18},{18... | collective-permute-start | bytes 393224 | tf_op jit(solution)/shard_map/while/body/eval_jaxpr/ppermute | solution.py:14
  180.1 6.8 %collective-permute-start.1 = (s32[128]{0:T(128)S(1)}, s32[128]{0:T(128)S(1)}, u32[]{:S(2)}, u32[]{:S(2)}) collective-permute-start(s32[128]{0:T(128)S(1)} %get-tuple-element.178), channel_id=1, source_target_pairs={{0,2},{2,4},{4,6},{6,8},{8,10},{10,12},{12,14},{14,16},{16,18},{18... | collective-permute-start | bytes 1544 | tf_op jit(solution)/shard_map/while/body/eval_jaxpr/ppermute | solution.py:14
  187.0 12.0 %collective-permute-start = (bf16[128,512]{1,0:T(8,128)(2,1)S(1)}, bf16[128,512]{1,0:T(8,128)(2,1)S(1)}, u32[]{:S(2)}, u32[]{:S(2)}) collective-permute-start(bf16[128,512]{1,0:T(8,128)(2,1)S(1)} %get-tuple-element.177), channel_id=1, source_target_pairs={{0,2},{2,4},{4,6},{6,8},{8,10},{10,12},{12,14},{14,16},{16,18},{18... | collective-permute-start | bytes 393224 | tf_op jit(solution)/shard_map/while/body/eval_jaxpr/ppermute | solution.py:14
  191.9 7.0 %collective-permute-start.1 = (s32[128]{0:T(128)S(1)}, s32[128]{0:T(128)S(1)}, u32[]{:S(2)}, u32[]{:S(2)}) collective-permute-start(s32[128]{0:T(128)S(1)} %get-tuple-element.178), channel_id=1, source_target_pairs={{0,2},{2,4},{4,6},{6,8},{8,10},{10,12},{12,14},{14,16},{16,18},{18... | collective-permute-start | bytes 1544 | tf_op jit(solution)/shard_map/while/body/eval_jaxpr/ppermute | solution.py:14
  (8 other events, 315.6 us)
Sparse Core Ops, SparseCore 0:
  10.3 45.8 all-gather.3
  58.5 57.4 all-gather.5
  118.3 58.7 all-gather.7
  216.4 20.0 reduce-scatter.1
where the time goes:
time: 246 us; the launch traced here: 245 us
  starting transfers between devices  126 us (51%)
  waiting for transfers between devices  56.4 us (23%)
  blocking collectives  21.8 us (9%)
  matrix products  15.9 us (6%)
  between operations  14 us (6%)
  other arithmetic  7.63 us (3%)
    ppermute x30, starting transfers between devices, from_behind(): return lax.ppermute(x, axis, pairs)  126 us
    all_gather x1, waiting for transfers between devices, per_device(): lax.all_gather(w_keyval, 'seq', axis=0, tiled=True)  22.2 us
    reduce_scatter x1, waiting for transfers between devices, per_device(): lax.psum_scatter(partial_value.astype(jnp.bfloat16), 'tp', scatter_dimens...  20.2 us
    psum x1, blocking collectives, per_device(): starts = lax.psum(below, 'seq')  13.8 us
    ppermute x30, waiting for transfers between devices, from_behind(): return lax.ppermute(x, axis, pairs)  11.9 us
    all_gather x1, blocking collectives, per_device(): gathered = lax.all_gather(tokens, 'tp', axis=1, tiled=True)  7.95 us
    dot_general x1, matrix products, per_device(): jnp.dot(attended, lax.all_gather(w_out, 'seq', axis=1, tiled=True), prefe...  5.25 us
  transfers between devices with their start and end apart: 34, of which 17 were waited for; matrix products, arithmetic and copies ran while one was open for 7% of the time, Pallas kernels for 0%

commit v1 on v0

--- a/solution.py
+++ b/solution.py
@@ -75,14 +75,20 @@
         store_seg = lax.dynamic_update_slice_in_dim(store_seg, current_seg[None], slot, 0)
         return (current, current_seg, store, store_seg)
 
-    store_init = jnp.zeros((reach, tok_rows, kv_cache.shape[1]), jnp.bfloat16)
-    seg_init = jnp.zeros((reach, tok_rows), jnp.int32)
-    final_state = lax.fori_loop(0, reach, advance, (kv_cache, seg_ids, store_init, seg_init))
-    block_kv = jnp.concatenate(
-        [final_state[2].reshape(reach * tok_rows, kv_cache.shape[1]), kv_cache], axis=0
-    )
-    block_seg = jnp.concatenate([final_state[3].reshape(reach * tok_rows), seg_ids], axis=0)
-    key_index = (my_index - reach) * tok_rows + jnp.arange((reach + 1) * tok_rows, dtype=jnp.int32)
+    if reach == seq_count - 1:
+        block_kv = lax.all_gather(kv_cache, "seq", axis=0, tiled=True)
+        block_seg = lax.all_gather(seg_ids, "seq", axis=0, tiled=True)
+        first_key = 0
+    else:
+        store_init = jnp.zeros((reach, tok_rows, kv_cache.shape[1]), jnp.bfloat16)
+        seg_init = jnp.zeros((reach, tok_rows), jnp.int32)
+        final_state = lax.fori_loop(0, reach, advance, (kv_cache, seg_ids, store_init, seg_init))
+        block_kv = jnp.concatenate(
+            [final_state[2].reshape(reach * tok_rows, kv_cache.shape[1]), kv_cache], axis=0
+        )
+        block_seg = jnp.concatenate([final_state[3].reshape(reach * tok_rows), seg_ids], axis=0)
+        first_key = (my_index - reach) * tok_rows
+    key_index = first_key + jnp.arange((reach + 1) * tok_rows, dtype=jnp.int32)
     live = (block_seg[None, :] == seg_ids[:, None]) & (key_index[None, :] <= token_index[:, None])
     live = live & (token_index[:, None] - key_index[None, :] < WINDOW) & (key_index[None, :] >= 0)
     all_keys = block_kv[:, :HD]

time: 246 us -> 241 us (0.980)
  starting transfers between devices: 126 us -> 0.19 us
  waiting for transfers between devices: 56.4 us -> 161 us
  blocking collectives: 21.8 us -> 40.7 us
    ppermute x30 -> x0, starting transfers between devices: 126 us -> none  [from_behind(): return lax.ppermute(x, axis, pairs)]
    all_gather x1, waiting for transfers between devices: 0.02 us -> 49.9 us  [per_device(): lax.all_gather(w_out, 'seq', axis=1, tiled=True)]
    all_gather x0 -> x1, waiting for transfers between devices: none -> 38.4 us  [per_device(): block_kv = lax.all_gather(kv_cache, 'seq', axis=0, tiled=True)]
    all_gather x1, waiting for transfers between devices: 0.01 us -> 33.2 us  [per_device(): lax.all_gather(w_query, 'seq', axis=0, tiled=True)]
    all_gather x0 -> x1, blocking collectives: none -> 19 us  [per_device(): block_seg = lax.all_gather(seg_ids, 'seq', axis=0, tiled=True)]
    ppermute x30 -> x0, waiting for transfers between devices: 11.9 us -> none  [from_behind(): return lax.ppermute(x, axis, pairs)]
    reduce_scatter x1, waiting for transfers between devices: 20.2 us -> 13.9 us  [per_device(): lax.psum_scatter(partial_value.astype(jnp.bfloat16), 'tp', scatter_dimens...]
  transfers between devices with their start and end apart: 34 -> 5, of which waited for: 17 -> 5; matrix products, arithmetic and copies ran while one was open for 7% -> 8% of each run, Pallas kernels for 0% -> 0%
where the time goes in v1:
time: 241 us
  waiting for transfers between devices  161 us (67%)
  blocking collectives  40.7 us (17%)
  matrix products  17.3 us (7%)
  between operations  13.9 us (6%)
  other arithmetic  6.85 us (3%)
    all_gather x1, waiting for transfers between devices, per_device(): lax.all_gather(w_out, 'seq', axis=1, tiled=True)  49.9 us
    all_gather x1, waiting for transfers between devices, per_device(): block_kv = lax.all_gather(kv_cache, 'seq', axis=0, tiled=True)  38.4 us
    all_gather x1, waiting for transfers between devices, per_device(): lax.all_gather(w_query, 'seq', axis=0, tiled=True)  33.2 us
    all_gather x1, waiting for transfers between devices, per_device(): lax.all_gather(w_keyval, 'seq', axis=0, tiled=True)  23.4 us
    all_gather x1, blocking collectives, per_device(): block_seg = lax.all_gather(seg_ids, 'seq', axis=0, tiled=True)  19 us
    reduce_scatter x1, waiting for transfers between devices, per_device(): lax.psum_scatter(partial_value.astype(jnp.bfloat16), 'tp', scatter_dimens...  13.9 us
    psum x1, blocking collectives, per_device(): starts = lax.psum(below, 'seq')  13.7 us
    all_gather x1, blocking collectives, per_device(): gathered = lax.all_gather(tokens, 'tp', axis=1, tiled=True)  7.95 us
  transfers between devices with their start and end apart: 5, of which 5 were waited for; matrix products, arithmetic and copies ran while one was open for 8% of the time, Pallas kernels for 0%

profile of v1, /device:TPU:0, one launch (start us, length us, event | category | flops | bytes accessed | tf_op | source)
XLA Modules:
  0.0 241.1 jit_solution(17121405719624229943)
XLA Ops:
  7.2 0.7 all-gather.8.cloned.1.call-update
  7.9 0.7 all-gather.6.cloned.1.call-update
  8.7 0.8 convert_reduce_fusion
  9.5 13.7 %psum.7 = s32[4]{0:T(128)S(1)} all-reduce(s32[4]{0:T(128)S(1)} %convert_reduce_fusion), channel_id=1, replica_groups=mesh['seq'=16,'tp'=2] {'seq'}, use_global_device_ids=true, to_apply=%region_2.0 | all-reduce | flops 4 | bytes 32 | tf_op jit(solution)/shard_map/psum | solution.py:50
  23.2 0.7 convert_element_type.59
  23.9 0.7 select_reduce_fusion
  24.6 8.0 %all_gather.19 = bf16[128,2560]{1,0:T(8,128)(2,1)S(1)} all-gather(bf16[128,1280]{1,0:T(8,128)(2,1)} %param.6), channel_id=1, replica_groups=mesh['seq'=16,'tp'=2] {'tp'}, dimensions={1}, use_global_device_ids=true | all-gather | bytes 983040 | tf_op jit(solution)/shard_map/all_gather | solution.py:45
  32.8 23.4 %all-gather.8.cloned.1.call-done = bf16[2560,512]{1,0:T(8,128)(2,1)} async-done(((bf16[160,512]{1,0:T(8,128)(2,1)}), bf16[2560,512]{1,0:T(8,128)(2,1)}) %all-gather.8.cloned.1.call-update) | async-done | bytes 2621456 | tf_op jit(solution)/shard_map/all_gather | solution.py:61
  56.2 2.9 %fusion.36 = f32[128,512]{0,1:T(8,128)S(1)} fusion(bf16[2560,512]{1,0:T(8,128)(2,1)} %all-gather.8.cloned.1.call-done, bf16[128,2560]{1,0:T(8,128)(2,1)S(1)} %all_gather.19, f32[2560]{0:T(1024)S(1)} %convert_element_type.59, f32[128]{0:T(128)S(1)} %add_rsqrt_fusion), kind=kOutput, calls=%fused_computation.62 | convolution fusion | flops 336855040 | bytes 3549696 | tf_op jit(solution)/shard_map/dot_general | solution.py:59
  59.4 0.7 pad_maximum_fusion.1
  60.1 0.5 all-gather.12.cloned.1.call-update
  60.7 19.0 %all-gather = s32[16,1,128]{2,1,0:T(1,128)S(1)} all-gather(s32[1,1,128]{2,1,0:T(1,128)S(1)} %bitcast.35), channel_id=1, replica_groups=mesh['seq'=16,'tp'=2] {'seq'}, dimensions={0}, use_global_device_ids=true | all-gather | bytes 8704 | tf_op jit(solution)/shard_map/all_gather | solution.py:80
  79.7 0.3 multiply_cosine_fusion
  80.0 33.2 %all-gather.6.cloned.1.call-done = bf16[2560,1024]{1,0:T(8,128)(2,1)} async-done(((bf16[160,1024]{1,0:T(8,128)(2,1)}), bf16[2560,1024]{1,0:T(8,128)(2,1)}) %all-gather.6.cloned.1.call-update) | async-done | bytes 5242896 | tf_op jit(solution)/shard_map/all_gather | solution.py:56
  113.2 3.4 %fusion.38 = f32[128,1024]{1,0:T(8,128)S(1)} fusion(bf16[2560,1024]{1,0:T(8,128)(2,1)} %all-gather.6.cloned.1.call-done, bf16[128,2560]{1,0:T(8,128)(2,1)S(1)} %all_gather.19, f32[2560]{0:T(1024)S(1)} %convert_element_type.59, f32[128]{0:T(128)S(1)} %add_rsqrt_fusion), kind=kOutput, calls=%fused_computation.63 | convolution fusion | flops 672399360 | bytes 6433280 | tf_op jit(solution)/shard_map/dot_general | solution.py:54
  117.4 38.4 %all-gather.10.cloned.1.call-done = bf16[2048,512]{0,1:T(8,128)(2,1)} async-done(((bf16[128,512]{0,1:T(8,128)(2,1)}), bf16[2048,512]{0,1:T(8,128)(2,1)}) %all-gather.10.cloned.1.call-update) | async-done | bytes 2097168 | tf_op jit(solution)/shard_map/all_gather | solution.py:79
  155.7 2.0 fusion.53
  158.0 0.6 fusion.52
  158.7 0.3 fusion.10
  159.0 0.6 fusion.51
  159.6 0.3 fusion.11
  159.9 0.6 fusion.50
  160.5 0.3 fusion.12
  160.8 0.5 convolution_convert_fusion.4
  161.3 0.5 convolution_convert_fusion.3
  161.8 0.5 convolution_convert_fusion.2
  162.3 0.5 convolution_convert_fusion.1
  162.9 49.9 %all-gather.12.cloned.1.call-done = bf16[1024,2560]{0,1:T(8,128)(2,1)} async-done(((bf16[1024,160]{0,1:T(8,128)(2,1)}), bf16[1024,2560]{0,1:T(8,128)(2,1)}) %all-gather.12.cloned.1.call-update) | async-done | bytes 5242896 | tf_op jit(solution)/shard_map/all_gather | solution.py:114
  212.8 5.2 %convolution_convert_fusion = bf16[128,2560]{1,0:T(8,128)(2,1)} fusion(bf16[1024,2560]{0,1:T(8,128)(2,1)} %all-gather.12.cloned.1.call-done, bf16[128,256]{1,0:T(8,128)(2,1)S(1)} %convolution_convert_fusion.1, bf16[128,256]{1,0:T(8,128)(2,1)S(1)} %convolution_convert_fusion.2, bf16[128,256]{1,0:T(8,128)(2,1)S(1)} %convolution_convert_fusion.3, ...), kind=kOutput, calls=%fused_computation | convolution fusion | flops 672464896 | bytes 6160384 | tf_op jit(solution)/shard_map/dot_general | solution.py:112
  218.0 0.8 copy.22
  218.8 13.9 %reduce-scatter.2.cloned.1.call-done = bf16[128,1280]{1,0:T(8,128)(2,1)} async-done(((bf16[128,2560]{1,0:T(8,128)(2,1)}), bf16[128,1280]{1,0:T(8,128)(2,1)}) %reduce-scatter.2.cloned.1.call-update) | async-done | bytes 327696 | tf_op jit(solution)/shard_map/reduce_scatter | solution.py:117
  232.8 1.8 add_convert_fusion
  (32 shorter events, 1.8 us)
Async XLA Ops:
  7.2 49.0 %all-gather.8.cloned.1.call-start = ((), (), s32[]{:S(2)}) async-start(), calls=%async_computation.2 | async-start | bytes 2785280 | tf_op jit(solution)/shard_map/all_gather | solution.py:61
  7.9 105.3 %all-gather.6.cloned.1.call-start = ((), (), s32[]{:S(2)}) async-start(), calls=%async_computation.1 | async-start | bytes 5570560 | tf_op jit(solution)/shard_map/all_gather | solution.py:56
  8.6 147.1 %all-gather.10.cloned.1.call-start = ((), (), s32[]{:S(2)}) async-start(), calls=%async_computation.3 | async-start | bytes 2228224 | tf_op jit(solution)/shard_map/all_gather | solution.py:79
  32.8 27.9 %copy-start.2 = (s32[128]{0:T(128)S(1)}, s32[128]{0:T(128)}, u32[]{:S(2)}) copy-start(s32[128]{0:T(128)} %param.7) | copy-start | bytes 1540
  60.1 152.7 %all-gather.12.cloned.1.call-start = ((), (), s32[]{:S(2)}) async-start(), calls=%async_computation.4 | async-start | bytes 5570560 | tf_op jit(solution)/shard_map/all_gather | solution.py:114
  60.7 172.1 %reduce-scatter.2.cloned.1.call-start = ((), (), s32[]{:S(2)}) async-start(), calls=%async_computation.5 | async-start | bytes 983040 | tf_op jit(solution)/shard_map/reduce_scatter | solution.py:117
  155.7 2.3 copy-start.3
  162.9 55.2 %copy-start.1 = (bf16[128,512]{0,1:T(8,128)(2,1)S(1)}, bf16[128,512]{0,1:T(8,128)(2,1)}, u32[]{:S(2)}) copy-start(bf16[128,512]{0,1:T(8,128)(2,1)} %pad_maximum_fusion.1) | copy-start | bytes 393220
  162.9 69.9 %copy-start = (bf16[128,1280]{1,0:T(8,128)(2,1)S(1)}, bf16[128,1280]{1,0:T(8,128)(2,1)}, u32[]{:S(2)}) copy-start(bf16[128,1280]{1,0:T(8,128)(2,1)} %param.6) | copy-start | bytes 983044
Sparse Core Ops, SparseCore 0:
  10.3 45.8 all-gather.7
  58.5 54.6 all-gather.5
  115.9 39.7 all-gather.9
  157.9 54.9 all-gather.11
  218.2 14.5 reduce-scatter.1

commit v2 on v1

--- a/solution.py
+++ b/solution.py
@@ -1,11 +1,14 @@
 import jax
 import jax.numpy as jnp
 from jax import lax
+from jax.experimental import pallas as pl
+from jax.experimental.pallas import tpu as pltpu
 from jax.sharding import PartitionSpec as P
 
 HD = 256
 WINDOW = 2048
 SEG_MEAN = 512
+CHUNK = 32
 
 
 def from_behind(x, axis, by):
@@ -121,9 +124,295 @@
     return (hidden, kv_cache)
 
 
+MESH = pl.DeviceIdType.MESH
+
+
+def block_kernel(
+    tok_ref, seg_ref, segcol_ref, gain_ref, freq_ref, wq_ref, wkv_ref, wo_ref,
+    hidden_ref, cache_ref,
+    tok, normed, seg, wkv, wq, wo, kv, half, queries, attended, partial, other,
+    local_sem, send_sem, recv_sem, pair_send, pair_recv,
+):
+    me = lax.axis_index("seq")
+    tp = lax.axis_index("tp")
+    z, x, c = me // 4, lax.rem(me // 2, 2), lax.rem(me, 2)
+    rows = tok_ref.shape[0]
+    width = tok_ref.shape[1]
+    shard = wq_ref.shape[0]
+    count = wq_ref.shape[1]
+    heads = count // HD
+    total = rows * 16
+
+    def index(zz, xx, cc):
+        return (zz * 2 + xx) * 2 + cc
+
+    z_peers = [index(lax.rem(z + k, 4), x, c) for k in (1, 2, 3)]
+    x_peer = index(z, 1 - x, c)
+    c_peer = index(z, x, 1 - c)
+
+    barrier = pltpu.get_barrier_semaphore()
+    for peer in z_peers + [x_peer, c_peer]:
+        pl.semaphore_signal(barrier, inc=1, device_id=(peer, tp), device_id_type=MESH)
+    pl.semaphore_signal(barrier, inc=1, device_id=(me, 1 - tp), device_id_type=MESH)
+
+    mine = [
+        pltpu.make_async_copy(wq_ref, wq.at[pl.ds(pl.multiple_of(me * shard, shard), shard)], local_sem.at[0]),
+        pltpu.make_async_copy(wo_ref, wo.at[pl.ds(pl.multiple_of(me * shard, shard), shard)], local_sem.at[1]),
+    ]
+    for copy in mine:
+        copy.start()
+    wkv[pl.ds(pl.multiple_of(me * shard, shard), shard), :] = jnp.where(
+        tp == 0, wkv_ref[:, :HD], wkv_ref[:, HD:]
+    )
+    seg[me] = seg_ref[...]
+    pl.semaphore_wait(barrier, 6)
+
+    def pair(which, src, dst):
+        return pltpu.make_async_remote_copy(
+            src_ref=src, dst_ref=dst, send_sem=pair_send.at[which], recv_sem=pair_recv.at[which],
+            device_id=(me, 1 - tp), device_id_type=MESH,
+        )
+
+    tok_copy = pair(0, tok_ref, tok.at[tp])
+    tok_copy.start()
+    tok[pl.ds(tp, 1)] = tok_ref[...][None]
+
+    steps = [(seg, 0, 0, 0), (wkv, shard, 0, shard)]
+    steps += [(wq, shard, at, CHUNK) for at in range(0, shard, CHUNK)]
+    steps += [(wo, shard, at, CHUNK) for at in range(0, shard, CHUNK)]
+    steps += [(kv, rows, 0, rows)]
+    per = shard // CHUNK
+    Q0, O0, KV = 2, 2 + per, 2 + 2 * per
+    sends = []
+
+    def view(s, slot):
+        buffer, each, at, size = steps[s]
+        if each == 0:
+            return buffer.at[slot]
+        return buffer.at[pl.ds(pl.multiple_of(slot * each + at, 16), size)]
+
+    def copy_of(s, slot, which, peer, src=None):
+        return pltpu.make_async_remote_copy(
+            src_ref=view(s, slot) if src is None else src, dst_ref=view(s, slot),
+            send_sem=send_sem.at[s, which], recv_sem=recv_sem.at[s, slot],
+            device_id=(peer, tp), device_id_type=MESH,
+        )
+
+    def push(s, slot, which, peer, src=None):
+        copy = copy_of(s, slot, which, peer, src)
+        copy.start()
+        sends.append(copy)
+
+    def own(s):
+        src = None
+        if Q0 <= s < O0:
+            src = wq_ref.at[pl.ds(steps[s][2], CHUNK)]
+        elif O0 <= s < KV:
+            src = wo_ref.at[pl.ds(steps[s][2], CHUNK)]
+        push(s, me, 3, x_peer, src)
+        for k in (0, 2, 1):
+            push(s, me, k, z_peers[k], src)
+        push(s, me, 4, c_peer, src)
+
+    def from_z(s):
+        for k in (2, 0, 1):
+            slot = z_peers[k]
+            copy_of(s, slot, 0, x_peer).wait_recv()
+            push(s, slot, 5 + k, x_peer)
+            push(s, slot, 8 + k, c_peer)
+
+    def from_x(s):
+        for k in range(4):
+            slot = index(lax.rem(z + k, 4), 1 - x, c)
+            copy_of(s, slot, 0, x_peer).wait_recv()
+            push(s, slot, 11 + k, c_peer)
+
+    def from_c(s):
+        for k in range(4):
+            for xx in range(2):
+                slot = index(lax.rem(z + k, 4), xx, 1 - c)
+                copy_of(s, slot, 0, c_peer).wait_recv()
+
+    own(0)
+    own(1)
+    own(Q0)
+    own(Q0 + 1)
+
+    tok_copy.wait_recv()
+    lower = tok[0].astype(jnp.float32)
+    upper = tok[1].astype(jnp.float32)
+    square = jnp.sum(lower * lower, axis=1, keepdims=True) + jnp.sum(upper * upper, axis=1, keepdims=True)
+    scale = lax.rsqrt(square / (2 * width) + 1e-06)
+    gain = gain_ref[...].astype(jnp.float32)
+    normed[:, :width] = (lower * scale * gain[:, :width]).astype(jnp.bfloat16)
+    normed[:, width:] = (upper * scale * gain[:, width:]).astype(jnp.bfloat16)
+
+    from_z(0)
+    own(Q0 + 2)
+    from_z(1)
+    from_x(0)
+    from_z(Q0)
+    from_x(1)
+    own(Q0 + 3)
+    from_c(0)
+
+    mine_seg = segcol_ref[...]
+    below = jnp.zeros((rows, rows), jnp.float32)
+    for slot in range(16):
+        below = below + (seg[slot] < mine_seg).astype(jnp.float32)
+    start = jnp.sum(below, axis=1, keepdims=True)
+    token_index = me * rows + lax.broadcasted_iota(jnp.int32, (rows, 1), 0)
+    angle = (token_index.astype(jnp.float32) - start) * freq_ref[...]
+    cosine = jnp.cos(angle)
+    sine = jnp.sin(angle)
+    lane = lax.broadcasted_iota(jnp.int32, angle.shape, 1)
+    sine = jnp.where(lane < HD // 4, -sine, sine)
+
+    def turn(part, cosine, sine):
+        return part * cosine + pltpu.roll(part, HD // 4, 1) * sine
+
+    from_z(Q0 + 1)
+    from_x(Q0)
+    own(Q0 + 4)
+    from_c(1)
+    raw = jnp.dot(normed[...], wkv[...], preferred_element_type=jnp.float32)
+    first = jnp.where(tp == 0, turn(raw[:, : HD // 2], cosine, sine), raw[:, : HD // 2])
+    half[pl.ds(tp, 1), :, : HD // 2] = first.astype(jnp.bfloat16)[None]
+    half[pl.ds(tp, 1), :, HD // 2 :] = raw[:, HD // 2 :].astype(jnp.bfloat16)[None]
+    half_copy = pair(1, half.at[tp], half.at[tp])
+    half_copy.start()
+    from_z(Q0 + 2)
+    from_x(Q0 + 1)
+    half_copy.wait_recv()
+    own_rows = pl.ds(pl.multiple_of(me * rows, rows), rows)
+    kv[own_rows, :HD] = half[0]
+    kv[own_rows, HD:] = half[1]
+    cache_ref[:, :HD] = half[0]
+    cache_ref[:, HD:] = half[1]
+    own(KV)
+    own(O0)
+    from_z(Q0 + 3)
+    from_x(Q0 + 2)
+    own(O0 + 1)
+    from_z(Q0 + 4)
+    from_x(Q0 + 3)
+    from_z(KV)
+    own(O0 + 2)
+    from_x(Q0 + 4)
+    from_z(O0)
+    from_x(KV)
+    for copy in mine:
+        copy.wait()
+    for at in range(per):
+        from_c(Q0 + at)
+
+    for head in range(heads):
+        raw = jnp.dot(normed[...], wq[:, head * HD : (head + 1) * HD], preferred_element_type=jnp.float32)
+        queries[:, head * HD : head * HD + HD // 2] = turn(raw[:, : HD // 2], cosine, sine).astype(jnp.bfloat16)
+        queries[:, head * HD + HD // 2 : (head + 1) * HD] = raw[:, HD // 2 :].astype(jnp.bfloat16)
+
+    own(O0 + 3)
+    from_z(O0 + 1)
+    from_x(O0)
+    from_c(KV)
+
+    def attend(head):
+        scores = lax.dot_general(
+            queries[:, head * HD : (head + 1) * HD], kv[:, :HD],
+            (((1,), (1,)), ((), ())), preferred_element_type=jnp.float32,
+        ) * HD ** (-0.5)
+        key_seg = jnp.concatenate([seg[slot] for slot in range(16)], axis=1)
+        key_index = lax.broadcasted_iota(jnp.int32, (1, total), 1)
+        live = (key_seg == mine_seg) & (key_index <= token_index) & (token_index - key_index < WINDOW)
+        scores = jnp.where(live, scores, -1e30)
+        peak = jnp.max(scores, axis=1, keepdims=True)
+        powered = jnp.exp(scores - peak)
+        weights = (powered / jnp.sum(powered, axis=1, keepdims=True)).astype(jnp.bfloat16)
+        attended[:, head * HD : (head + 1) * HD] = jnp.dot(
+            weights, kv[:, HD:], preferred_element_type=jnp.float32
+        ).astype(jnp.bfloat16)
+
+    for at in range(max(heads, per)):
+        if at < heads:
+            attend(at)
+        if 4 + at < per:
+            own(O0 + 4 + at)
+        if 2 + at < per:
+            from_z(O0 + 2 + at)
+        if 1 + at < per:
+            from_x(O0 + 1 + at)
+    for at in range(per):
+        from_c(O0 + at)
+
+    def project(which):
+        rows_of = pl.ds(pl.multiple_of(which * width, 256), width)
+        return lax.dot_general(
+            attended[...], wo[rows_of, :], (((1,), (1,)), ((), ())), preferred_element_type=jnp.float32
+        ).astype(jnp.bfloat16)
+
+    partial[...] = project(1 - tp)
+    out_copy = pair(2, partial, other)
+    out_copy.start()
+    own_part = project(tp).astype(jnp.float32)
+    out_copy.wait_recv()
+    summed = own_part + other[...].astype(jnp.float32)
+    hidden_ref[...] = (tok_ref[...].astype(jnp.float32) + summed).astype(jnp.bfloat16)
+
+    for copy in sends + [tok_copy, half_copy, out_copy]:
+        copy.wait_send()
+
+
+def per_device_kernel(tokens, seg_ids, norm_gain, w_query, w_keyval, w_out):
+    rows, width = tokens.shape
+    shard, count = w_query.shape
+    model = shard * 16
+    quarter = HD // 4
+    freq = 10000.0 ** (-jnp.arange(quarter, dtype=jnp.float32) / quarter)
+    freq = jnp.concatenate([freq, freq]).reshape(1, 2 * quarter)
+    steps = 3 + 2 * (shard // CHUNK)
+    vmem = pl.BlockSpec(memory_space=pltpu.VMEM)
+    bf16 = jnp.bfloat16
+    return pl.pallas_call(
+        block_kernel,
+        out_shape=(
+            jax.ShapeDtypeStruct((rows, width), bf16),
+            jax.ShapeDtypeStruct((rows, 2 * HD), bf16),
+        ),
+        in_specs=[vmem] * 8,
+        out_specs=(vmem, vmem),
+        scratch_shapes=[
+            pltpu.VMEM((2, rows, width), bf16),
+            pltpu.VMEM((rows, model), bf16),
+            pltpu.VMEM((16, 1, rows), jnp.int32),
+            pltpu.VMEM((model, HD), bf16),
+            pltpu.VMEM((model, count), bf16),
+            pltpu.VMEM((model, count), bf16),
+            pltpu.VMEM((16 * rows, 2 * HD), bf16),
+            pltpu.VMEM((2, rows, HD), bf16),
+            pltpu.VMEM((rows, count), bf16),
+            pltpu.VMEM((rows, count), bf16),
+            pltpu.VMEM((rows, width), bf16),
+            pltpu.VMEM((rows, width), bf16),
+            pltpu.SemaphoreType.DMA((2,)),
+            pltpu.SemaphoreType.DMA((steps, 15)),
+            pltpu.SemaphoreType.DMA((steps, 16)),
+            pltpu.SemaphoreType.DMA((3,)),
+            pltpu.SemaphoreType.DMA((3,)),
+        ],
+        compiler_params=pltpu.CompilerParams(
+            collective_id=0, has_side_effects=True, vmem_limit_bytes=48 * 1024 * 1024
+        ),
+    )(
+        tokens, seg_ids.reshape(1, rows), seg_ids.reshape(rows, 1), norm_gain.reshape(1, model), freq,
+        w_query, w_keyval, w_out.T,
+    )
+
+
 def solution(mesh):
     in_specs = (P("seq", "tp"), P("seq"), P(), P("seq", "tp"), P("seq", None), P("tp", "seq"))
     out_specs = (P("seq", "tp"), P("seq", None))
+    fits = mesh.shape["seq"] == 16 and mesh.shape["tp"] == 2
     return jax.shard_map(
-        per_device, mesh=mesh, in_specs=in_specs, out_specs=out_specs, check_vma=False
-    )
+        per_device_kernel if fits else per_device,
+        mesh=mesh, in_specs=in_specs, out_specs=out_specs, check_vma=False,
+    )

time: 241 us -> 111 us (0.46)
  waiting for transfers between devices: 161 us -> 0 us
  Pallas kernels: 0 us -> 103 us
  blocking collectives: 40.7 us -> 0 us
  matrix products: 17.3 us -> 0 us
  between operations: 13.9 us -> 0.66 us
  other arithmetic: 6.85 us -> 0.09 us
  local copies, waits for them, and re-layouts: 1.34 us -> 6.57 us
    all_gather x4 -> x0, waiting for transfers between devices: 145 us -> none  [the longest x1 49.9 us: per_device(): lax.all_gather(w_out, 'seq', axis=1, tiled=True)]
    pallas_call x0 -> x1, Pallas kernels: none -> 103 us  [per_device_kernel(): pl.pallas_call(block_kernel, out_shape=(jax.ShapeDtypeStruct((rows, width...]
    all_gather x2 -> x0, blocking collectives: 27 us -> none  [the longest x1 19 us: per_device(): block_seg = lax.all_gather(seg_ids, 'seq', axis=0, tiled=True)]
    dot_general x11 -> x0, matrix products: 17.3 us -> none  [the longest x1 5.18 us: per_device(): jnp.dot(attended, lax.all_gather(w_out, 'seq', axis=1, tiled=True), prefe...]
    reduce_scatter x1 -> x0, waiting for transfers between devices: 13.9 us -> none  [per_device(): lax.psum_scatter(partial_value.astype(jnp.bfloat16), 'tp', scatter_dimens...]
    psum x1 -> x0, blocking collectives: 13.7 us -> none  [per_device(): starts = lax.psum(below, 'seq')]
    unnamed x10 -> x14, local copies, waits for them, and re-layouts: 0.81 us -> 6.45 us
    reduce_sum x7 -> x0, other arithmetic: 2.96 us -> none  [the longest x4 1.23 us: per_device(): jnp.sum(powered, axis=1, keepdims=True)]
  transfers between devices with their start and end apart: 5 -> 0, of which waited for: 5 -> 0; matrix products, arithmetic and copies ran while one was open for 8% -> 0% of each run, Pallas kernels for 0% -> 0%
where the time goes in v2:
time: 111 us; the launch traced here: 110 us
  Pallas kernels  103 us (93%)
  local copies, waits for them, and re-layouts  6.57 us (6%)
    pallas_call x1, Pallas kernels, per_device_kernel(): pl.pallas_call(block_kernel, out_shape=(jax.ShapeDtypeStruct((rows, width...  103 us
    unnamed x14, local copies, waits for them, and re-layouts  6.45 us

profile of v2, /device:TPU:0, one launch (start us, length us, event | category | flops | bytes accessed | tf_op | source)
XLA Modules:
  0.0 110.3 jit_solution(5606406634135630625)
XLA Ops:
  0.6 0.0 copy-start.5
  0.7 0.1 maximum_bitcast_fusion.freq_ref
  0.7 0.6 copy-done.5
  1.3 0.0 copy-start.4
  1.3 0.6 copy-done.4
  2.0 0.1 copy.8.segcol_ref
  2.1 0.0 copy-start
  2.1 1.0 copy-done
  3.1 0.0 copy-start.1
  3.1 1.0 copy-done.1
  4.0 0.0 copy-start.2
  4.0 1.0 copy-done.2
  5.0 0.0 copy-start.3
  5.0 0.9 copy-done.3
  5.9 103.0 %shard_map.77 = (bf16[128,1280]{1,0:T(8,128)(2,1)S(1)}, bf16[128,512]{1,0:T(8,128)(2,1)S(1)}) custom-call(bf16[128,1280]{1,0:T(8,128)(2,1)S(1)} %copy-done, s32[1,128]{1,0:T(1,128)S(1)} %bitcast.7, s32[128,1]{1,0:T(8,128)S(1)} %copy.8.segcol_ref, bf16[1,2560]{1,0:T(2,128)(2,1)S(1)} %reshape.18.gain_ref, f32[1,128]{1,0:T(1,128)S(1)} %maximum_bitcast_fusion.freq_ref, ...), custom_call_target="tpu_custom_call" | custom-call | tf_op jit(solution)/shard_map/pallas_call | solution.py:375
  108.9 0.7 copy.11
  109.6 0.7 copy.12
  (2 shorter events, 0.0 us)
Async XLA Ops:
  0.6 0.7 copy-start.5
  1.3 0.7 copy-start.4
  2.1 1.0 copy-start
  3.1 1.0 copy-start.1
  4.0 1.0 copy-start.2
  5.0 0.9 copy-start.3

commit v3 on v2

--- a/solution.py
+++ b/solution.py
@@ -9,6 +9,7 @@
 WINDOW = 2048
 SEG_MEAN = 512
 CHUNK = 32
+ACROSS = 99
 
 
 def from_behind(x, axis, by):
@@ -130,7 +131,7 @@
 def block_kernel(
     tok_ref, seg_ref, segcol_ref, gain_ref, freq_ref, wq_ref, wkv_ref, wo_ref,
     hidden_ref, cache_ref,
-    tok, normed, seg, wkv, wq, wo, kv, half, queries, attended, partial, other,
+    tok, normed, seg, wkv, wq, wo, kv, queries, attended, partial, other,
     local_sem, send_sem, recv_sem, pair_send, pair_recv,
 ):
     me = lax.axis_index("seq")
@@ -147,6 +148,9 @@
         return (zz * 2 + xx) * 2 + cc
 
     z_peers = [index(lax.rem(z + k, 4), x, c) for k in (1, 2, 3)]
+    low = z - 1 + 2 * (1 - (z + 3) // 4)
+    far = 3 * (1 - z // 2)
+    origins = (low, 6 - z - low - far, far)
     x_peer = index(z, 1 - x, c)
     c_peer = index(z, x, 1 - c)
 
@@ -180,9 +184,11 @@
     steps = [(seg, 0, 0, 0), (wkv, shard, 0, shard)]
     steps += [(wq, shard, at, CHUNK) for at in range(0, shard, CHUNK)]
     steps += [(wo, shard, at, CHUNK) for at in range(0, shard, CHUNK)]
-    steps += [(kv, rows, 0, rows)]
+    steps += [(kv.at[tp], rows, 0, rows), (kv.at[1 - tp], rows, 0, rows)]
     per = shard // CHUNK
-    Q0, O0, KV = 2, 2 + per, 2 + 2 * per
+    Q0, O0, KV, KY = 2, 2 + per, 2 + 2 * per, 3 + 2 * per
+    across = (Q0 + ACROSS, O0 + ACROSS)
+    used = [0] * len(steps)
     sends = []
 
     def view(s, slot):
@@ -191,17 +197,40 @@
             return buffer.at[slot]
         return buffer.at[pl.ds(pl.multiple_of(slot * each + at, 16), size)]
 
-    def copy_of(s, slot, which, peer, src=None):
-        return pltpu.make_async_remote_copy(
+    def arrived(s, slot):
+        pltpu.make_async_remote_copy(
+            src_ref=view(s, slot), dst_ref=view(s, slot),
+            send_sem=send_sem.at[s, 0], recv_sem=recv_sem.at[s, slot],
+            device_id=(x_peer, tp), device_id_type=MESH,
+        ).wait_recv()
+
+    def push(s, slot, peer, src=None, when=None, land=None, plane=None):
+        which = used[s]
+        used[s] += 1
+        copy = pltpu.make_async_remote_copy(
             src_ref=view(s, slot) if src is None else src, dst_ref=view(s, slot),
-            send_sem=send_sem.at[s, which], recv_sem=recv_sem.at[s, slot],
-            device_id=(peer, tp), device_id_type=MESH,
+            send_sem=send_sem.at[s, which], recv_sem=recv_sem.at[s if land is None else land, slot],
+            device_id=(peer, tp if plane is None else plane), device_id_type=MESH,
         )
-
-    def push(s, slot, which, peer, src=None):
-        copy = copy_of(s, slot, which, peer, src)
-        copy.start()
-        sends.append(copy)
+        if when is None:
+            copy.start()
+        else:
+            pl.when(when)(copy.start)
+        sends.append((copy, when))
+
+    up, down = me + 4, me - 4
+
+    def both_ways(s, slot, src=None):
+        push(s, slot, up, src, when=z < 3)
+        push(s, slot, down, src, when=z > 0)
+
+    def onward(s, slot, origin):
+        push(s, slot, up, when=(origin < z) & (z < 3))
+        push(s, slot, down, when=(origin > z) & (z > 0))
+
+    def to_plane(s, slot):
+        if s == KV:
+            push(s, slot, me, land=KY, plane=1 - tp)
 
     def own(s):
         src = None
@@ -209,34 +238,64 @@
             src = wq_ref.at[pl.ds(steps[s][2], CHUNK)]
         elif O0 <= s < KV:
             src = wo_ref.at[pl.ds(steps[s][2], CHUNK)]
-        push(s, me, 3, x_peer, src)
-        for k in (0, 2, 1):
-            push(s, me, k, z_peers[k], src)
-        push(s, me, 4, c_peer, src)
+        to_plane(s, me)
+        push(s, me, x_peer, src)
+        both_ways(s, me, src)
+        push(s, me, c_peer, src)
+        if s in across:
+            slot = index(z, 1 - x, c)
+            late.append((s, slot))
+
+    late = []
+
+    def turn_late():
+        while late:
+            s, slot = late.pop(0)
+            arrived(s, slot)
+            both_ways(s, slot)
+            push(s, slot, c_peer)
 
     def from_z(s):
-        for k in (2, 0, 1):
-            slot = z_peers[k]
-            copy_of(s, slot, 0, x_peer).wait_recv()
-            push(s, slot, 5 + k, x_peer)
-            push(s, slot, 8 + k, c_peer)
+        turn_late()
+        for origin in origins:
+            slot = index(origin, x, c)
+            arrived(s, slot)
+            onward(s, slot, origin)
+            if s not in across:
+                push(s, slot, x_peer)
+            to_plane(s, slot)
+            push(s, slot, c_peer)
+            if s in across:
+                slot = index(origin, 1 - x, c)
+                arrived(s, slot)
+                onward(s, slot, origin)
+                push(s, slot, c_peer)
 
     def from_x(s):
+        if s in across:
+            return
         for k in range(4):
             slot = index(lax.rem(z + k, 4), 1 - x, c)
-            copy_of(s, slot, 0, x_peer).wait_recv()
-            push(s, slot, 11 + k, c_peer)
+            arrived(s, slot)
+            to_plane(s, slot)
+            push(s, slot, c_peer)
+
+    def from_y():
+        for k in range(4):
+            for k2 in range(2):
+                slot = index(lax.rem(z + k, 4), lax.rem(x + k2, 2), c)
+                arrived(KY, slot)
+                push(KY, slot, c_peer)
 
     def from_c(s):
         for k in range(4):
             for xx in range(2):
-                slot = index(lax.rem(z + k, 4), xx, 1 - c)
-                copy_of(s, slot, 0, c_peer).wait_recv()
+                arrived(s, index(lax.rem(z + k, 4), xx, 1 - c))
 
     own(0)
     own(1)
-    own(Q0)
-    own(Q0 + 1)
+    for at in range(per):
+        own(Q0 + at)
 
     tok_copy.wait_recv()
     lower = tok[0].astype(jnp.float32)
@@ -248,12 +307,10 @@
     normed[:, width:] = (upper * scale * gain[:, width:]).astype(jnp.bfloat16)
 
     from_z(0)
-    own(Q0 + 2)
     from_z(1)
     from_x(0)
     from_z(Q0)
     from_x(1)
-    own(Q0 + 3)
     from_c(0)
 
     mine_seg = segcol_ref[...]
@@ -273,32 +330,26 @@
 
     from_z(Q0 + 1)
     from_x(Q0)
-    own(Q0 + 4)
     from_c(1)
     raw = jnp.dot(normed[...], wkv[...], preferred_element_type=jnp.float32)
     first = jnp.where(tp == 0, turn(raw[:, : HD // 2], cosine, sine), raw[:, : HD // 2])
-    half[pl.ds(tp, 1), :, : HD // 2] = first.astype(jnp.bfloat16)[None]
-    half[pl.ds(tp, 1), :, HD // 2 :] = raw[:, HD // 2 :].astype(jnp.bfloat16)[None]
-    half_copy = pair(1, half.at[tp], half.at[tp])
-    half_copy.start()
+    own_rows = pl.ds(pl.multiple_of(me * rows, rows), rows)
+    kv[pl.ds(tp, 1), own_rows, : HD // 2] = first.astype(jnp.bfloat16)[None]
+    kv[pl.ds(tp, 1), own_rows, HD // 2 :] = raw[:, HD // 2 :].astype(jnp.bfloat16)[None]
+    own(KV)
+    own(O0)
     from_z(Q0 + 2)
     from_x(Q0 + 1)
-    half_copy.wait_recv()
-    own_rows = pl.ds(pl.multiple_of(me * rows, rows), rows)
-    kv[own_rows, :HD] = half[0]
-    kv[own_rows, HD:] = half[1]
-    cache_ref[:, :HD] = half[0]
-    cache_ref[:, HD:] = half[1]
-    own(KV)
-    own(O0)
+    own(O0 + 1)
     from_z(Q0 + 3)
     from_x(Q0 + 2)
-    own(O0 + 1)
+    own(O0 + 2)
     from_z(Q0 + 4)
     from_x(Q0 + 3)
+    own(O0 + 3)
     from_z(KV)
-    own(O0 + 2)
     from_x(Q0 + 4)
+    own(O0 + 4)
     from_z(O0)
     from_x(KV)
     for copy in mine:
@@ -311,14 +362,19 @@
         queries[:, head * HD : head * HD + HD // 2] = turn(raw[:, : HD // 2], cosine, sine).astype(jnp.bfloat16)
         queries[:, head * HD + HD // 2 : (head + 1) * HD] = raw[:, HD // 2 :].astype(jnp.bfloat16)
 
-    own(O0 + 3)
     from_z(O0 + 1)
     from_x(O0)
+    from_y()
+    from_z(O0 + 2)
+    from_x(O0 + 1)
     from_c(KV)
+    from_c(KY)
+    cache_ref[:, :HD] = kv[0, own_rows, :]
+    cache_ref[:, HD:] = kv[1, own_rows, :]
 
     def attend(head):
         scores = lax.dot_general(
-            queries[:, head * HD : (head + 1) * HD], kv[:, :HD],
+            queries[:, head * HD : (head + 1) * HD], kv[0],
             (((1,), (1,)), ((), ())), preferred_element_type=jnp.float32,
         ) * HD ** (-0.5)
         key_seg = jnp.concatenate([seg[slot] for slot in range(16)], axis=1)
@@ -329,18 +385,16 @@
         powered = jnp.exp(scores - peak)
         weights = (powered / jnp.sum(powered, axis=1, keepdims=True)).astype(jnp.bfloat16)
         attended[:, head * HD : (head + 1) * HD] = jnp.dot(
-            weights, kv[:, HD:], preferred_element_type=jnp.float32
+            weights, kv[1], preferred_element_type=jnp.float32
         ).astype(jnp.bfloat16)
 
     for at in range(max(heads, per)):
         if at < heads:
             attend(at)
-        if 4 + at < per:
-            own(O0 + 4 + at)
+        if 3 + at < per:
+            from_z(O0 + 3 + at)
         if 2 + at < per:
-            from_z(O0 + 2 + at)
-        if 1 + at < per:
-            from_x(O0 + 1 + at)
+            from_x(O0 + 2 + at)
     for at in range(per):
         from_c(O0 + at)
 
@@ -351,15 +405,20 @@
         ).astype(jnp.bfloat16)
 
     partial[...] = project(1 - tp)
-    out_copy = pair(2, partial, other)
+    out_copy = pair(1, partial, other)
     out_copy.start()
     own_part = project(tp).astype(jnp.float32)
     out_copy.wait_recv()
     summed = own_part + other[...].astype(jnp.float32)
     hidden_ref[...] = (tok_ref[...].astype(jnp.float32) + summed).astype(jnp.bfloat16)
 
-    for copy in sends + [tok_copy, half_copy, out_copy]:
+    for copy in [tok_copy, out_copy]:
         copy.wait_send()
+    for copy, when in sends:
+        if when is None:
+            copy.wait_send()
+        else:
+            pl.when(when)(copy.wait_send)
 
 
 def per_device_kernel(tokens, seg_ids, norm_gain, w_query, w_keyval, w_out):
@@ -369,7 +428,7 @@
     quarter = HD // 4
     freq = 10000.0 ** (-jnp.arange(quarter, dtype=jnp.float32) / quarter)
     freq = jnp.concatenate([freq, freq]).reshape(1, 2 * quarter)
-    steps = 3 + 2 * (shard // CHUNK)
+    steps = 4 + 2 * (shard // CHUNK)
     vmem = pl.BlockSpec(memory_space=pltpu.VMEM)
     bf16 = jnp.bfloat16
     return pl.pallas_call(
@@ -387,17 +446,16 @@
             pltpu.VMEM((model, HD), bf16),
             pltpu.VMEM((model, count), bf16),
             pltpu.VMEM((model, count), bf16),
-            pltpu.VMEM((16 * rows, 2 * HD), bf16),
-            pltpu.VMEM((2, rows, HD), bf16),
+            pltpu.VMEM((2, 16 * rows, HD), bf16),
             pltpu.VMEM((rows, count), bf16),
             pltpu.VMEM((rows, count), bf16),
             pltpu.VMEM((rows, width), bf16),
             pltpu.VMEM((rows, width), bf16),
             pltpu.SemaphoreType.DMA((2,)),
-            pltpu.SemaphoreType.DMA((steps, 15)),
+            pltpu.SemaphoreType.DMA((steps, 32)),
             pltpu.SemaphoreType.DMA((steps, 16)),
-            pltpu.SemaphoreType.DMA((3,)),
-            pltpu.SemaphoreType.DMA((3,)),
+            pltpu.SemaphoreType.DMA((2,)),
+            pltpu.SemaphoreType.DMA((2,)),
         ],
         compiler_params=pltpu.CompilerParams(
             collective_id=0, has_side_effects=True, vmem_limit_bytes=48 * 1024 * 1024

time: 111 us -> 107 us (0.964)
  Pallas kernels: 103 us -> 99.2 us
    pallas_call x1, Pallas kernels: 103 us -> 99.2 us  [per_device_kernel(): pl.pallas_call(block_kernel, out_shape=(jax.ShapeDtypeStruct((rows, width...]
where the time goes in v3:
time: 107 us
  Pallas kernels  99.2 us (93%)
  local copies, waits for them, and re-layouts  6.57 us (6%)
    pallas_call x1, Pallas kernels, per_device_kernel(): pl.pallas_call(block_kernel, out_shape=(jax.ShapeDtypeStruct((rows, width...  99.2 us
    unnamed x14, local copies, waits for them, and re-layouts  6.45 us

profile of v3, /device:TPU:0, one launch (start us, length us, event | category | flops | bytes accessed | tf_op | source)
XLA Modules:
  0.0 106.6 jit_solution(14034853364433055285)
XLA Ops:
  0.6 0.0 copy-start.5
  0.7 0.1 maximum_bitcast_fusion.freq_ref
  0.7 0.6 copy-done.5
  1.3 0.0 copy-start.4
  1.3 0.6 copy-done.4
  2.0 0.1 copy.8.segcol_ref
  2.1 0.0 copy-start
  2.1 1.0 copy-done
  3.1 0.0 copy-start.1
  3.1 1.0 copy-done.1
  4.0 0.0 copy-start.2
  4.0 1.0 copy-done.2
  5.0 0.0 copy-start.3
  5.0 0.9 copy-done.3
  5.9 99.2 %shard_map.77 = (bf16[128,1280]{1,0:T(8,128)(2,1)S(1)}, bf16[128,512]{1,0:T(8,128)(2,1)S(1)}) custom-call(bf16[128,1280]{1,0:T(8,128)(2,1)S(1)} %copy-done, s32[1,128]{1,0:T(1,128)S(1)} %bitcast.7, s32[128,1]{1,0:T(8,128)S(1)} %copy.8.segcol_ref, bf16[1,2560]{1,0:T(2,128)(2,1)S(1)} %reshape.18.gain_ref, f32[1,128]{1,0:T(1,128)S(1)} %maximum_bitcast_fusion.freq_ref, ...), custom_call_target="tpu_custom_call" | custom-call | tf_op jit(solution)/shard_map/pallas_call | solution.py:434
  105.2 0.7 copy.11
  105.9 0.7 copy.12
  (2 shorter events, 0.0 us)
Async XLA Ops:
  0.6 0.7 copy-start.5
  1.3 0.7 copy-start.4
  2.1 1.0 copy-start
  3.1 1.0 copy-start.1
  4.0 1.0 copy-start.2
  5.0 0.9 copy-start.3
